TPU v7x, 128 devices: a whole 4x4x4 slice. The times are simulated.
128 devices in a mesh: section: 8 (over y, x_lo), tp: 16 (over z, x_hi, core).
Axes of the slice: x: 4 (x_hi: 2, x_lo: 2; x = x_hi * 2 + x_lo), y: 4, z: 4, core: 2. Of those that a mesh axis runs over, the one named last changes fastest.
Arguments:
- hidden: bfloat16 [8, 256, 8192], P('section', 'tp'), may hold values from -4 to 4
- tiles: bfloat16 [256, 8192], P(('section', 'tp')), may hold values from -8 to 8
- tile_counts: int32 [4], replicated, may hold values from 1 to 4, 8 in all
- sample_order: int32 [4], replicated, may hold values from 0 to 3, each once
- query_weight: bfloat16 [8, 8192, 8192], P('section', None, 'tp'), may hold values from -0.0625 to 0.0625
- tile_weight: bfloat16 [8, 8192, 2048], P('section', None, 'tp'), may hold values from -0.0625 to 0.0625
- output_weight: bfloat16 [8, 8192, 8192], P('section', 'tp'), may hold values from -0.0625 to 0.0625
- head_gains: float32 [8, 2, 128], P('section'), may hold values from 0.5 to 2
- cross_gate: float32 [8], P('section'), may hold values from 0.5 to 2
- cotangent: bfloat16 [8, 256, 8192], P('section', 'tp'), may hold values from -3 to 3
Outputs:
- out_hidden: bfloat16 [8, 256, 8192], P('section', 'tp')
- hidden_grad: bfloat16 [8, 256, 8192], P('section', 'tp')
- tile_grad: float32 [256, 8192], P(('section', 'tp'))
Inputs may be any that keep to these rules, and one draw needn't show every extreme that they name: tile_counts add up to 8; sample s's tiles follow those of samples 0 to s - 1 in the packed tile rows. `sample_order`: every sample appears once.
All inputs are finite; a program needn't handle non-finite values.
Results may differ from a plain program's by a relative error of at most 0.018.
Values may be sent and summed in bfloat16 or wider, within the bound.
A program may use at most 128 MiB of HBM per device.

v0:
```python
import jax
import jax.numpy as jnp
from jax import lax
from jax.sharding import PartitionSpec as P

LEN = 64
PATCH = 32
SAMPLES = 4
TOK = 256
TILE_ROWS = 256


NORM_EPS = 1e-06


def partner(block, axis, distance):
    count = lax.axis_size(axis)
    route = []
    for low in range(count):
        high = low | 1 << distance
        if high != low and high < count:
            route += [(low, high), (high, low)]
    return lax.ppermute(block, axis, route)


def head_norm(values, gain):
    scale = lax.rsqrt(jnp.mean(values * values, axis=-1, keepdims=True) + NORM_EPS)
    return (values * scale * gain, scale)


def head_norm_back(values, scale, gain, grad):
    normed = values * scale
    scaled = grad * gain
    return scale * (scaled - normed * jnp.mean(normed * scaled, axis=-1, keepdims=True))


def widen(values):
    return lax.optimization_barrier(values).astype(jnp.float32)


def linked_rows(tile_counts, sample_order):
    ends = jnp.cumsum(tile_counts)
    tile_index = jnp.arange(TILE_ROWS, dtype=jnp.int32) // PATCH
    tile_sample = jnp.sum((tile_index[:, None] >= ends[None, :]).astype(jnp.int32), axis=1)
    position = jnp.arange(TOK, dtype=jnp.int32) // LEN
    picks = position[:, None] == jnp.arange(SAMPLES, dtype=jnp.int32)[None, :]
    token_sample = jnp.sum(jnp.where(picks, sample_order[None, :], 0), axis=1)
    return token_sample[:, None] == tile_sample[None, :]


def contract_last(left, right):
    return lax.dot_general(
        left, right, (((1,), (1,)), ((), ())), preferred_element_type=jnp.float32
    )


def body(
    hidden,
    tiles,
    tile_counts,
    sample_order,
    query_weight,
    tile_weight,
    output_weight,
    head_gains,
    cross_gate,
    cotangent,
):
    text_rows = hidden[0]
    grad_rows = cotangent[0]
    query_local = query_weight[0]
    tile_local = tile_weight[0]
    output_local = output_weight[0]
    gains = head_gains[0]
    gate = jnp.tanh(cross_gate[0])
    head_size = gains.shape[1]
    local_heads = query_local.shape[1] // head_size
    is_even = lax.axis_index("tp") % 2 == 0
    query_gain = gains[0] * head_size ** (-0.5)
    key_gain = gains[1]
    linked = linked_rows(tile_counts, sample_order)
    queries = jnp.dot(
        lax.all_gather(text_rows, "tp", axis=0, tiled=True),
        query_local,
        preferred_element_type=jnp.float32,
    ).reshape(TOK, local_heads, head_size)
    query_normed, query_scale = head_norm(queries, query_gain)
    normed_queries = query_normed.astype(jnp.bfloat16)
    projected = jnp.dot(
        lax.all_gather(tiles, ("section", "tp"), axis=0, tiled=True),
        tile_local,
        preferred_element_type=jnp.float32,
    )
    key_normed, key_scale = head_norm(projected, key_gain)
    outgoing = jnp.where(is_even, key_normed, projected).astype(jnp.bfloat16)
    incoming = partner(outgoing, "tp", 0)
    keys = jnp.where(is_even, outgoing, incoming)
    values = jnp.where(is_even, incoming, outgoing)
    scores = jnp.einsum("thd,rd->htr", normed_queries, keys, preferred_element_type=jnp.float32)
    raised = jnp.where(linked[None], jnp.exp(scores), 0.0)
    weights = (raised / jnp.sum(raised, axis=-1, keepdims=True)).astype(jnp.bfloat16)
    attended = jnp.einsum("htr,rd->thd", weights, values, preferred_element_type=jnp.float32)
    attended = attended.astype(jnp.bfloat16).reshape(TOK, local_heads * head_size)
    block = attended
    branch = lax.psum_scatter(
        (gate * jnp.dot(block, output_local, preferred_element_type=jnp.float32)).astype(
            jnp.bfloat16
        ),
        "tp",
        scatter_dimension=0,
        tiled=True,
    ).astype(jnp.float32)
    out_hidden = (text_rows.astype(jnp.float32) + branch).astype(jnp.bfloat16)
    grad_out = (
        (gate * contract_last(lax.all_gather(grad_rows, "tp", axis=0, tiled=True), output_local))
        .astype(jnp.bfloat16)
        .reshape(TOK, local_heads, head_size)
    )
    grad_prob = jnp.einsum("thd,rd->htr", grad_out, values, preferred_element_type=jnp.float32)
    weights_full = widen(weights)
    center = jnp.sum(weights_full * grad_prob, axis=-1, keepdims=True)
    grad_score = (weights_full * (grad_prob - center)).astype(jnp.bfloat16)
    grad_normed = jnp.einsum("htr,rd->thd", grad_score, keys, preferred_element_type=jnp.float32)
    grad_query = head_norm_back(queries, query_scale, query_gain, grad_normed).astype(jnp.bfloat16)
    grad_query = grad_query.reshape(TOK, local_heads * head_size)
    block = grad_query
    grad_input = lax.psum_scatter(
        contract_last(block, query_local).astype(jnp.bfloat16),
        "tp",
        scatter_dimension=0,
        tiled=True,
    ).astype(jnp.float32)
    hidden_grad = (grad_rows.astype(jnp.float32) + grad_input).astype(jnp.bfloat16)
    grad_keys = jnp.einsum(
        "htr,thd->rd", grad_score, normed_queries, preferred_element_type=jnp.float32
    ).astype(jnp.bfloat16)
    grad_values = jnp.einsum(
        "htr,thd->rd", weights, grad_out, preferred_element_type=jnp.float32
    ).astype(jnp.bfloat16)
    outgoing_grad = jnp.where(is_even, grad_values, grad_keys)
    incoming_grad = partner(outgoing_grad, "tp", 0)
    own_key = head_norm_back(projected, key_scale, key_gain, widen(grad_keys)).astype(jnp.bfloat16)
    other_key = head_norm_back(projected, key_scale, key_gain, widen(incoming_grad)).astype(
        jnp.bfloat16
    )
    first = jnp.where(is_even, own_key, grad_values)
    second = jnp.where(is_even, other_key, incoming_grad)
    tile_grad = lax.psum_scatter(
        contract_last(first, tile_local) + contract_last(second, tile_local),
        ("section", "tp"),
        scatter_dimension=0,
        tiled=True,
    )
    return (out_hidden[None], hidden_grad[None], tile_grad)


def solution(mesh):
    placed = (
        P("section", "tp", None),
        P(("section", "tp"), None),
        P(),
        P(),
        P("section", None, "tp"),
        P("section", None, "tp"),
        P("section", "tp", None),
        P("section", None, None),
        P("section"),
        P("section", "tp", None),
    )
    return jax.shard_map(
        body,
        mesh=mesh,
        in_specs=placed,
        out_specs=(P("section", "tp", None), P("section", "tp", None), P(("section", "tp"), None)),
        check_vma=False,
    )
```

profile of v0, /device:TPU:1, one launch (start us, length us, event | category | flops | bytes accessed | tf_op | source)
XLA Modules:
  0.0 687.7 jit_solution(8329860036445100564)
XLA Ops:
  7.2 0.0 copy-start
  7.2 0.0 all-gather.7.cloned.1.call-start
  7.2 0.7 all-gather.7.cloned.1.call-update
  7.9 0.0 all-gather.9.cloned.1.call-start
  8.0 0.7 all-gather.9.cloned.1.call-update
  8.7 0.0 all-gather.11.cloned.1.call-start
  8.7 0.7 all-gather.11.cloned.1.call-update
  9.4 0.0 all-reduce.3.cloned.1.call-start
  9.5 0.0 copy-start.13
  9.5 0.0 copy-start.12
  9.5 0.0 copy-start.11
  9.5 11.4 %copy.55 = bf16[512,8192]{1,0:T(8,128)(2,1)} copy(bf16[512,8192]{0,1:T(8,128)(2,1)} %bitcast.122) | data formatting | bytes 16777216 | tf_op jit(solution)/shard_map/dot_general | solution.py:82
  20.9 0.2 reduce-window.8
  21.8 0.1 convert_reduce_fusion
  21.9 0.0 copy-done.11
  21.9 0.1 broadcast_compare_fusion
  22.0 47.5 %all-gather.7.cloned.1.call-done = bf16[1,256,8192]{2,1,0:T(8,128)(2,1)} async-done(((bf16[1,16,8192]{2,1,0:T(8,128)(2,1)}), bf16[1,256,8192]{2,1,0:T(8,128)(2,1)}) %all-gather.7.cloned.1.call-update) | async-done | bytes 4194320 | tf_op jit(solution)/shard_map/all_gather | solution.py:83
  69.6 7.0 %multiply_reduce_fusion.1 = (f32[256,4]{0,1:T(4,128)S(1)}, f32[256,4,128]{0,2,1:T(8,128)S(1)}) fusion(bf16[4,128,8192]{2,1,0:T(8,128)(2,1)} %bitcast.123, bf16[1,256,8192]{2,1,0:T(8,128)(2,1)} %all-gather.7.cloned.1.call-done), kind=kOutput, calls=%fused_computation.43 | convolution fusion | flops 2147744768 | bytes 13111296 | tf_op jit(solution)/shard_map/dot_general | solution.py:82
  76.6 48.6 %all-gather.9.cloned.1.call-done = bf16[1,256,8192]{2,1,0:T(8,128)(2,1)} async-done(((bf16[1,16,8192]{2,1,0:T(8,128)(2,1)}), bf16[1,256,8192]{2,1,0:T(8,128)(2,1)}) %all-gather.9.cloned.1.call-update) | async-done | bytes 4194320 | tf_op jit(solution)/shard_map/all_gather | solution.py:115
  125.3 7.7 %fusion.26 = bf16[32,4,8,128]{3,2,1,0:T(8,128)(2,1)} fusion(bf16[1,512,8192]{2,1,0:T(8,128)(2,1)} %param.16, bf16[1,256,8192]{2,1,0:T(8,128)(2,1)} %all-gather.9.cloned.1.call-done, f32[]{:T(128)} %bitcast.1), kind=kOutput, calls=%fused_computation.27 | convolution fusion | flops 2147745792 | bytes 12845060 | tf_op jit(solution)/shard_map/dot_general | solution.py:52
  133.0 189.0 %all-gather.11.cloned.1.call-done = bf16[128,2,8192]{2,1,0:T(2,128)(2,1)} async-done(((bf16[1,2,8192]{2,1,0:T(2,128)(2,1)}), bf16[128,2,8192]{2,1,0:T(2,128)(2,1)}) %all-gather.11.cloned.1.call-update) | async-done | bytes 4194320 | tf_op jit(solution)/shard_map/all_gather | solution.py:90
  322.0 7.2 %reshape.139 = bf16[256,8192]{1,0:T(8,128)(2,1)} reshape(bf16[128,2,8192]{2,1,0:T(2,128)(2,1)} %all-gather.11.cloned.1.call-done) | data formatting | bytes 8388608
  329.2 0.0 copy-done
  329.2 3.7 multiply_reduce_fusion.4
  332.9 0.1 select_convert_fusion
  333.0 0.0 copy-start.6
  333.1 1.2 collective-permute-start
  334.3 0.1 multiply_convert_fusion.1
  334.4 0.0 copy-done.6
  334.4 0.8 collective-permute-done
  335.2 0.1 broadcast_select_fusion.1
  335.3 0.5 copy-done.9
  335.8 0.6 copy-done.4
  336.4 1.3 fusion.14
  337.7 1.3 divide_convert_fusion
  339.1 1.5 fusion.33
  340.6 1.2 fusion.34
  341.8 0.9 fusion.31
  342.7 2.1 broadcast_select_fusion
  344.8 0.4 collective-permute-start.1
  345.2 0.9 collective-permute-done.1
  346.1 1.0 multiply_reduce_fusion.2
  347.1 2.2 fusion.9
  349.3 4.7 convolution_add_fusion
  354.0 0.0 all-reduce.3.cloned.1.call-update
  354.0 0.2 reduce-scatter.3.cloned.1.call-start
  354.2 0.6 copy-done.7
  354.8 0.0 copy-done.10
  354.9 1.9 convolution_convert_fusion.1
  356.8 7.7 %fusion = bf16[256,8192]{1,0:T(8,128)(2,1)} fusion(bf16[256,512]{0,1:T(8,128)(2,1)S(1)} %bitcast.124, bf16[1,512,8192]{2,1,0:T(8,128)(2,1)} %param.16, f32[]{:T(128)} %bitcast.1), kind=kOutput, calls=%fused_computation.2 | convolution fusion | flops 2151677952 | bytes 12845060 | tf_op jit(solution)/shard_map/dot_general | solution.py:106
  364.5 0.0 reduce-scatter.3.cloned.1.call-update
  364.6 0.0 reduce-scatter.5.cloned.1.call-start
  364.6 0.3 multiply_reduce_fusion
  364.9 0.1 multiply_convert_fusion
  365.0 0.0 copy-start.2
  365.0 0.0 copy-start.3
  365.0 8.1 %convolution_convert_fusion = bf16[256,8192]{1,0:T(8,128)(2,1)} fusion(bf16[256,512]{0,1:T(8,128)(2,1)S(1)} %bitcast.125, bf16[1,8192,512]{2,1,0:T(8,128)(2,1)} %param.14), kind=kOutput, calls=%fused_computation.3 | convolution fusion | flops 2149580800 | bytes 12845056 | tf_op jit(solution)/shard_map/dot_general | solution.py:52
  373.1 0.0 reduce-scatter.5.cloned.1.call-update
  373.1 140.6 %all-reduce.3.cloned.1.call-done = f32[256,8192]{1,0:T(8,128)} async-done(((f32[256,8192]{1,0:T(8,128)}), f32[256,8192]{1,0:T(8,128)}) %all-reduce.3.cloned.1.call-update) | async-done | bytes 8388624
  513.7 1.6 constant_dynamic-slice_fusion
  515.3 80.5 %reduce-scatter.3.cloned.1.call-done = bf16[16,8192]{1,0:T(8,128)(2,1)} async-done(((bf16[256,8192]{1,0:T(8,128)(2,1)}), bf16[16,8192]{1,0:T(8,128)(2,1)}) %reduce-scatter.3.cloned.1.call-update) | async-done | bytes 262160 | tf_op jit(solution)/shard_map/reduce_scatter | solution.py:105
  595.8 1.7 fusion.38
  597.5 81.6 %reduce-scatter.5.cloned.1.call-done = bf16[16,8192]{1,0:T(8,128)(2,1)} async-done(((bf16[256,8192]{1,0:T(8,128)(2,1)}), bf16[16,8192]{1,0:T(8,128)(2,1)}) %reduce-scatter.5.cloned.1.call-update) | async-done | bytes 262160 | tf_op jit(solution)/shard_map/reduce_scatter | solution.py:127
  679.2 1.7 fusion.39
  (22 shorter events, 0.1 us)
Async XLA Ops:
  7.2 322.1 %copy-start = (bf16[1,8192,128]{2,1,0:T(8,128)(2,1)S(1)}, bf16[1,8192,128]{2,1,0:T(8,128)(2,1)}, u32[]{:S(2)}) copy-start(bf16[1,8192,128]{2,1,0:T(8,128)(2,1)} %param.15) | copy-start | bytes 6291460
  7.2 62.4 %all-gather.7.cloned.1.call-start = ((), (), s32[]{:S(2)}) async-start(), calls=%async_computation.4 | async-start | bytes 4456448 | tf_op jit(solution)/shard_map/all_gather | solution.py:83
  7.9 117.4 %all-gather.9.cloned.1.call-start = ((), (), s32[]{:S(2)}) async-start(), calls=%async_computation.5 | async-start | bytes 4456448 | tf_op jit(solution)/shard_map/all_gather | solution.py:115
  8.7 313.3 %all-gather.11.cloned.1.call-start = ((), (), s32[]{:S(2)}) async-start(), calls=%async_computation.6 | async-start | bytes 4227072 | tf_op jit(solution)/shard_map/all_gather | solution.py:90
  9.4 504.3 %all-reduce.3.cloned.1.call-start = ((), (), s32[]{:S(2)}) async-start(), calls=%async_computation.7 | async-start | bytes 16777216
  9.5 11.5 %copy-start.13 = (s32[4]{0:T(128)S(1)}, s32[4]{0:T(128)}, u32[]{:S(2)}) copy-start(s32[4]{0:T(128)} %param.12) | copy-start | bytes 52
  9.5 12.3 %copy-start.12 = (s32[4]{0:T(128)S(1)}, s32[4]{0:T(128)}, u32[]{:S(2)}) copy-start(s32[4]{0:T(128)} %param.13) | copy-start | bytes 52
  9.5 12.4 %copy-start.11 = (f32[1,2,128]{2,1,0:T(2,128)S(1)}, f32[1,2,128]{2,1,0:T(2,128)}, u32[]{:S(2)}) copy-start(f32[1,2,128]{2,1,0:T(2,128)} %param.17) | copy-start | bytes 3076
  22.0 313.2 %copy-start.8 = (pred[256,256]{0,1:T(8,128)(4,1)}, pred[256,256]{0,1:T(8,128)(4,1)S(1)}, u32[]{:S(2)}) copy-start(pred[256,256]{0,1:T(8,128)(4,1)S(1)} %broadcast_compare_fusion) | copy-start | bytes 196612
  333.0 1.3 copy-start.6
  333.1 2.1 collective-permute-start
  335.2 0.6 copy-start.9
  335.8 0.6 copy-start.4
  339.1 1.5 copy-start.1
  344.8 1.3 collective-permute-start.1
  354.0 0.8 copy-start.7
  354.0 0.9 copy-start.10
  354.0 241.8 %reduce-scatter.3.cloned.1.call-start = ((), (), s32[]{:S(2)}) async-start(), calls=%async_computation.2 | async-start | bytes 4456448 | tf_op jit(solution)/shard_map/reduce_scatter | solution.py:105
  356.8 7.8 %copy-start.5 = (bf16[256,128]{0,1:T(8,128)(2,1)S(1)}, bf16[256,128]{0,1:T(8,128)(2,1)}, u32[]{:S(2)}) copy-start(bf16[256,128]{0,1:T(8,128)(2,1)} %copy-done.4) | copy-start | bytes 196612
  364.6 314.6 %reduce-scatter.5.cloned.1.call-start = ((), (), s32[]{:S(2)}) async-start(), calls=%async_computation.3 | async-start | bytes 4456448 | tf_op jit(solution)/shard_map/reduce_scatter | solution.py:127
  365.0 230.8 %copy-start.2 = (bf16[1,16,8192]{2,1,0:T(8,128)(2,1)S(1)}, bf16[1,16,8192]{2,1,0:T(8,128)(2,1)}, u32[]{:S(2)}) copy-start(bf16[1,16,8192]{2,1,0:T(8,128)(2,1)} %param.10) | copy-start | bytes 786436
  365.0 314.2 %copy-start.3 = (bf16[1,16,8192]{2,1,0:T(8,128)(2,1)S(1)}, bf16[1,16,8192]{2,1,0:T(8,128)(2,1)}, u32[]{:S(2)}) copy-start(bf16[1,16,8192]{2,1,0:T(8,128)(2,1)} %param.19) | copy-start | bytes 786436
Sparse Core Ops, SparseCore 0:
  10.5 59.0 all-gather.6
  72.1 53.1 all-gather.8
  127.0 194.9 all-gather.10
  354.1 159.5 all-reduce.2
  518.1 77.6 reduce-scatter.2
  599.7 79.4 reduce-scatter.4
where the time goes:
time: 689 us; the launch traced here: 688 us
  waiting for transfers between devices  592 us (86%)
  matrix products  50.5 us (7%)
  local copies, waits for them, and re-layouts  22.1 us (3%)
  between operations  15.1 us (2%)
    all_gather x1, waiting for transfers between devices, body(): lax.all_gather(tiles, ('section', 'tp'), axis=0, tiled=True)  189 us
    unnamed x7, waiting for transfers between devices  143 us
    reduce_scatter x1, waiting for transfers between devices, body(): lax.psum_scatter(contract_last(block, query_local).astype(jnp.bfloat16),...  81.6 us
    reduce_scatter x1, waiting for transfers between devices, body(): lax.psum_scatter((gate * jnp.dot(block, output_local, preferred_element_t...  80.5 us
    all_gather x1, waiting for transfers between devices, body(): lax.all_gather(grad_rows, 'tp', axis=0, tiled=True)  48.6 us
    all_gather x1, waiting for transfers between devices, body(): lax.all_gather(text_rows, 'tp', axis=0, tiled=True)  47.5 us
    dot_general x4, matrix products, contract_last(): lax.dot_general(left, right, (((1,), (1,)), ((), ())), preferred_element_...  22.7 us
  transfers between devices with their start and end apart: 8, of which 8 were waited for; matrix products, arithmetic and copies ran while one was open for 7% of the time, Pallas kernels for 0%

commit v1 on v0

v1 whole, which is shorter than its diff:
```python
import functools
import jax
import jax.numpy as jnp
from jax import lax
from jax.experimental import pallas as pl
from jax.experimental.pallas import tpu as pltpu
from jax.sharding import PartitionSpec as P

MESH = pl.DeviceIdType.MESH
NORM_EPS = 1e-06
D = 8192
HD = 128
LOCAL = 512
HEADS = 4
ROWS = 256
BF = jnp.bfloat16
F32 = jnp.float32

XZ = ((0, 2304, 768), (2304, 2304, 768))
ZX = ((4608, 1792, 896), (6400, 1792, 896))
PIECE = 512


def contract_last(left, right):
    return lax.dot_general(left, right, (((1,), (1,)), ((), ())), preferred_element_type=F32)


def contract_first(left, right):
    return lax.dot_general(left, right, (((0,), (0,)), ((), ())), preferred_element_type=F32)


def norm_scale(values):
    return lax.rsqrt(jnp.mean(values * values, axis=-1, keepdims=True) + NORM_EPS)


def head_norm_back(values, scale, gain, grad):
    normed = values * scale
    scaled = grad * gain
    return scale * (scaled - normed * jnp.mean(normed * scaled, axis=-1, keepdims=True))


def add_to(total, *terms):
    value = total[...].astype(F32)
    for term in terms:
        value = value + term[...].astype(F32)
    total[...] = value.astype(total.dtype)


def kernel(
    counts, order, gate_ref, gains, hid, cot, til, wq_hbm, wt_hbm, wo_hbm,
    out_ref, grad_ref, tgrad_ref,
    wq, wt, wo, hfull, cfull, tfull,
    sib_o, rel_o, zin_o, xin_o,
    sib_g, rel_g, zin_g, xin_g,
    sib_t, yrel, yin, xin_t, zin_t,
    tin, flat, block, gin,
    queries, gradout, normedq, weights, attended, gradq, proj, kv, gxin, gxout, mask,
    load_sem, send_sem, recv_sem,
):
    sec = lax.axis_index("section")
    tp = lax.axis_index("tp")
    y, xl = lax.div(sec, 2), lax.rem(sec, 2)
    z, xh, c = lax.div(tp, 4), lax.rem(lax.div(tp, 2), 2), lax.rem(tp, 2)
    x = xh * 2 + xl
    zh, zl = lax.div(z, 2), lax.rem(z, 2)
    member = lax.rem(tp, 8)
    oc, ox = 1 - c, 1 - xh

    def turn(value, by):
        return lax.rem(value + by, 4)

    def device(dx=0, dy=0, dz=0, core=None):
        nx, ny, nz = turn(x, dx), turn(y, dy), turn(z, dz)
        core = c if core is None else core
        return (ny * 2 + lax.rem(nx, 2), nz * 4 + lax.div(nx, 2) * 2 + core)

    def mate(step):
        return lax.rem(member + step, 8)

    sib = device(core=oc)
    xpair = device(dx=2)
    zup, zdown, zfar = device(dz=1), device(dz=3), device(dz=2)
    yup, ydown = device(dy=1), device(dy=3)
    xup, xdown = device(dx=1), device(dx=3)

    loads = []
    for i, (src, dst) in enumerate(((wq_hbm, wq), (wt_hbm, wt), (wo_hbm, wo))):
        loads.append(pltpu.make_async_copy(src, dst, load_sem.at[i]))
        loads[-1].start()

    barrier = pltpu.get_barrier_semaphore()
    zodd = device(dz=lax.rem(zl * 2 + 3, 4))
    greeted = [(sec, zh * 8 + mate(step)) for step in range(1, 8)]
    greeted += [zodd, zfar, yup, ydown, xup, xdown]
    for other in greeted:
        pl.semaphore_signal(barrier, inc=1, device_id=other, device_id_type=MESH)

    hfull[c, z, xh] = hid[...]
    cfull[c, z, xh] = cot[...]

    tile_index = lax.div(lax.broadcasted_iota(jnp.int32, (1, ROWS), 1), 32)
    tile_sample = jnp.zeros((1, ROWS), jnp.int32)
    end = jnp.int32(0)
    for i in range(4):
        end = end + counts[i]
        tile_sample = tile_sample + (tile_index >= end).astype(jnp.int32)
    for i in range(4):
        row = (tile_sample == order[i]).astype(F32)
        for half in range(2):
            mask[pl.ds(half * 128 + i * 32, 32), :] = jnp.broadcast_to(row, (32, ROWS))
    gate = jnp.tanh(jnp.full((1, HD), gate_ref[0], F32))
    query_gain = gains[0:1, :] * HD ** (-0.5)
    key_gain = gains[1:2, :]

    pl.semaphore_wait(barrier, len(greeted))

    used = [0]

    def send(src, dst, target):
        i = used[0]
        used[0] += 1
        copy = pltpu.make_async_remote_copy(
            src_ref=src, dst_ref=dst, send_sem=send_sem.at[i], recv_sem=recv_sem.at[i],
            device_id=target, device_id_type=MESH,
        )
        copy.start()
        return copy

    def here(ref, target):
        return send(ref, ref, target)

    def sent(copies):
        for copy in copies:
            copy.wait_send()

    def gather_xz(full, part, use):
        col, width, _ = part
        cols = pl.ds(col, width)
        low, high = pl.ds(col, width // 2), pl.ds(col + width // 2, width // 2)
        a = here(full.at[c, z, xh, :, cols], xpair)
        yield
        a.wait_recv()
        up = here(full.at[c, z, :, :, cols], zup)
        down = here(full.at[c, z, :, :, cols], zdown)
        yield
        up.wait_recv()
        up2 = here(full.at[c, turn(z, 3), :, :, low], zup)
        down.wait_recv()
        down2 = here(full.at[c, turn(z, 1), :, :, high], zdown)
        yield
        up2.wait_recv()
        down2.wait_recv()
        s = here(full.at[c, :, :, :, cols], sib)
        yield
        s.wait_recv()
        use(part)
        sent([a, up, down, up2, down2, s])
        yield

    def gather_zx(full, part, use):
        col, width, _ = part
        cols = pl.ds(col, width)
        low, high = pl.ds(col, width // 2), pl.ds(col + width // 2, width // 2)
        mine = full.at[c, z, xh, :, cols]
        up, down, a = here(mine, zup), here(mine, zdown), here(mine, xpair)
        yield
        up.wait_recv()
        up2 = here(full.at[c, turn(z, 3), xh, :, low], zup)
        a1 = here(full.at[c, turn(z, 3), xh, :, cols], xpair)
        down.wait_recv()
        down2 = here(full.at[c, turn(z, 1), xh, :, high], zdown)
        a2 = here(full.at[c, turn(z, 1), xh, :, cols], xpair)
        yield
        up2.wait_recv()
        down2.wait_recv()
        a3 = here(full.at[c, turn(z, 2), xh, :, cols], xpair)
        yield
        for copy in (a, a1, a2, a3):
            copy.wait_recv()
        s = here(full.at[c, :, :, :, cols], sib)
        yield
        s.wait_recv()
        use(part)
        sent([up, down, a, up2, a1, down2, a2, a3, s])
        yield

    def use_hidden(part):
        col, width, step = part

        def one(i, carry):
            at = pl.ds(pl.multiple_of(col + i * step, 128), step)
            rows = hfull[:, :, :, :, at].reshape(ROWS, step)
            queries[...] += jnp.dot(rows, wq[at, :], preferred_element_type=F32)
            return carry

        lax.fori_loop(0, width // step, one, 0)

    def use_cot(part):
        col, width, step = part

        def one(i, carry):
            at = pl.ds(pl.multiple_of(col + i * step, 128), step)
            rows = cfull[:, :, :, :, at].reshape(ROWS, step)
            gradout[...] += contract_last(rows, wo[:, at])
            return carry

        lax.fori_loop(0, width // step, one, 0)

    def tblock(full, yy, xx):
        return full.at[c, yy, lax.div(xx, 2), lax.rem(xx, 2)]

    def gather_tiles():
        copies = []
        for step in range(1, 8):
            j = mate(step)
            copies.append(send(til.at[j], tin.at[step], (sec, zh * 8 + j)))
        yield
        for copy in copies:
            copy.wait_recv()
        tin[0] = til[member]
        for s in range(8):
            owner = lax.rem(member + 8 - s, 8)
            flat[pl.ds(pl.multiple_of(owner * 16, 16), 16), :] = tin[s].astype(F32)
        for r in range(2):
            for b in range(8):
                block[b, pl.ds(r, 8, stride=2), :] = flat[pl.ds(r * 8 + b, 8, stride=16), :]
        own = tfull.at[c, y, xh, xl, zh, zl]
        for b in range(8):
            own[:, pl.ds(b * 128, 128)] = block[b].astype(BF)
        zs = [here(own, zup), here(own, zdown), here(own, zfar)]
        yield
        for copy in zs:
            copy.wait_recv()
        mine = tblock(tfull, y, x)
        xs = [here(mine, xup), here(mine, xdown), here(mine, xpair)]
        ups, downs = [here(mine, yup)], [here(mine, ydown)]
        yield
        for copy, by in zip(xs, (3, 1, 2)):
            copy.wait_recv()
            got = tblock(tfull, y, turn(x, by))
            ups.append(here(got, yup))
            downs.append(here(got, ydown))
        sibs = [here(tfull.at[c, y], sib)]
        yield
        far = []
        for k, by in enumerate((0, 3, 1, 2)):
            ups[k].wait_recv()
            downs[k].wait_recv()
            if k % 2 == 0:
                far.append(here(tblock(tfull, turn(y, 3), turn(x, by)), yup))
            else:
                far.append(here(tblock(tfull, turn(y, 1), turn(x, by)), ydown))
        sibs.append(here(tfull.at[c, turn(y, 3)], sib))
        sibs.append(here(tfull.at[c, turn(y, 1)], sib))
        yield
        for copy in far:
            copy.wait_recv()
        sibs.append(here(tfull.at[c, turn(y, 2)], sib))
        yield
        for copy in sibs:
            copy.wait_recv()
        sent(copies + zs + xs + ups + downs + far + sibs)
        yield

    def scatter_xz(full, sibin, rel, zin, xin, part, make, finish):
        col, width, _ = part
        cols = pl.ds(col, width)
        low, high = pl.ds(col, width // 2), pl.ds(col + width // 2, width // 2)
        make(part)
        s = send(full.at[oc, :, :, :, cols], sibin.at[:, :, :, cols], sib)
        yield
        s.wait_recv()
        add_to(full.at[c, turn(z, 2), :, :, cols], sibin.at[turn(z, 2), :, :, cols])
        r0 = send(full.at[c, turn(z, 2), :, :, low], rel.at[0, :, :, low], zup)
        r1 = send(full.at[c, turn(z, 2), :, :, high], rel.at[1, :, :, high], zdown)
        for by in (1, 3, 0):
            add_to(full.at[c, turn(z, by), :, :, cols], sibin.at[turn(z, by), :, :, cols])
        yield
        r0.wait_recv()
        add_to(full.at[c, turn(z, 1), :, :, low], rel.at[0, :, :, low])
        z0 = send(full.at[c, turn(z, 1), :, :, cols], zin.at[0, :, :, cols], zup)
        r1.wait_recv()
        add_to(full.at[c, turn(z, 3), :, :, high], rel.at[1, :, :, high])
        z1 = send(full.at[c, turn(z, 3), :, :, cols], zin.at[1, :, :, cols], zdown)
        yield
        z0.wait_recv()
        z1.wait_recv()
        add_to(full.at[c, z, ox, :, cols], zin.at[0, ox, :, cols], zin.at[1, ox, :, cols])
        a = send(full.at[c, z, ox, :, cols], xin.at[0, :, cols], xpair)
        yield
        a.wait_recv()
        finish(cols, (full.at[c, z, xh, :, cols], zin.at[0, xh, :, cols], zin.at[1, xh, :, cols], xin.at[0, :, cols]))
        sent([s, r0, r1, z0, z1, a])
        yield

    def scatter_zx(full, sibin, rel, zin, xin, part, make, finish):
        col, width, _ = part
        cols = pl.ds(col, width)
        low, high = pl.ds(col, width // 2), pl.ds(col + width // 2, width // 2)
        make(part)
        s = send(full.at[oc, :, :, :, cols], sibin.at[:, :, :, cols], sib)
        yield
        s.wait_recv()
        add_to(full.at[c, :, ox, :, cols], sibin.at[:, ox, :, cols])
        a = send(full.at[c, :, ox, :, cols], xin.at[:, :, cols], xpair)
        yield
        a.wait_recv()
        add_to(full.at[c, turn(z, 2), xh, :, cols], sibin.at[turn(z, 2), xh, :, cols], xin.at[turn(z, 2), :, cols])
        r0 = send(full.at[c, turn(z, 2), xh, :, low], rel.at[0, 0, :, low], zup)
        r1 = send(full.at[c, turn(z, 2), xh, :, high], rel.at[1, 0, :, high], zdown)
        for by in (1, 3):
            add_to(full.at[c, turn(z, by), xh, :, cols], sibin.at[turn(z, by), xh, :, cols], xin.at[turn(z, by), :, cols])
        yield
        r0.wait_recv()
        add_to(full.at[c, turn(z, 1), xh, :, low], rel.at[0, 0, :, low])
        z0 = send(full.at[c, turn(z, 1), xh, :, cols], zin.at[0, 0, :, cols], zup)
        r1.wait_recv()
        add_to(full.at[c, turn(z, 3), xh, :, high], rel.at[1, 0, :, high])
        z1 = send(full.at[c, turn(z, 3), xh, :, cols], zin.at[1, 0, :, cols], zdown)
        yield
        z0.wait_recv()
        z1.wait_recv()
        finish(cols, (full.at[c, z, xh, :, cols], sibin.at[z, xh, :, cols], xin.at[z, :, cols], zin.at[0, 0, :, cols], zin.at[1, 0, :, cols]))
        sent([s, a, r0, r1, z0, z1])
        yield

    def total(terms):
        value = terms[0][...].astype(F32)
        for term in terms[1:]:
            value = value + term[...].astype(F32)
        return value

    def make_out(part):
        col, width, _ = part

        def one(i, carry):
            at = pl.ds(pl.multiple_of(col + i * 256, 128), 256)
            value = jnp.dot(attended[...], wo[:, at], preferred_element_type=F32)
            hfull[:, :, :, :, at] = value.astype(BF).reshape(2, 4, 2, 16, 256)
            return carry

        lax.fori_loop(0, width // 256, one, 0)

    def finish_out(cols, terms):
        out_ref[:, cols] = (hid[:, cols].astype(F32) + gate[0:1, 0:1] * total(terms)).astype(BF)

    def make_grad(part):
        col, width, _ = part

        def one(i, carry):
            at = pl.ds(pl.multiple_of(col + i * 256, 128), 256)
            value = contract_last(gradq[...], wq[at, :])
            cfull[:, :, :, :, at] = value.astype(BF).reshape(2, 4, 2, 16, 256)
            return carry

        lax.fori_loop(0, width // 256, one, 0)

    def finish_grad(cols, terms):
        grad_ref[:, cols] = (cot[:, cols].astype(F32) + total(terms)).astype(BF)

    def scatter_tiles(col):
        cols = pl.ds(col, PIECE)

        def unit(ref, *index):
            return ref.at[(*index, Ellipsis, cols)]

        for core in (oc, c):
            for h in range(2):
                for l in range(2):
                    at = (l * 4 + h * 2 + core) * 1024 + col
                    value = contract_last(gxout[...], wt[pl.ds(pl.multiple_of(at, 128), PIECE), :])
                    tfull[core, :, h, :, :, l, :, cols] = value.astype(BF).reshape(4, 2, 2, 16, PIECE)
            if core is oc:
                s = send(tfull.at[oc, :, :, :, :, :, :, cols], sib_t.at[:, :, :, :, :, :, cols], sib)
        yield
        s.wait_recv()

        def merge(by):
            yy = turn(y, by)
            for h in range(2):
                add_to(tfull.at[c, yy, h, :, :, :, :, cols], sib_t.at[yy, h, :, :, :, :, cols])

        merge(2)
        r0 = send(tfull.at[c, turn(y, 2), 0, :, :, :, :, cols], yrel.at[0, :, :, :, :, cols], yup)
        r1 = send(tfull.at[c, turn(y, 2), 1, :, :, :, :, cols], yrel.at[1, :, :, :, :, cols], ydown)
        for by in (1, 3, 0):
            merge(by)
        yield
        r0.wait_recv()
        add_to(tfull.at[c, turn(y, 1), 0, :, :, :, :, cols], yrel.at[0, :, :, :, :, cols])
        y0 = send(tfull.at[c, turn(y, 1), :, :, :, :, :, cols], yin.at[0, :, :, :, :, :, cols], yup)
        r1.wait_recv()
        add_to(tfull.at[c, turn(y, 3), 1, :, :, :, :, cols], yrel.at[1, :, :, :, :, cols])
        y1 = send(tfull.at[c, turn(y, 3), :, :, :, :, :, cols], yin.at[1, :, :, :, :, :, cols], ydown)
        yield
        y0.wait_recv()
        y1.wait_recv()
        xs = []
        for k, (by, target) in enumerate(((2, xpair), (1, xup), (3, xdown), (0, None))):
            h, l = lax.div(turn(x, by), 2), lax.rem(turn(x, by), 2)
            add_to(
                tfull.at[c, y, h, l, :, :, :, cols],
                yin.at[0, h, l, :, :, :, cols],
                yin.at[1, h, l, :, :, :, cols],
            )
            if target is not None:
                xs.append(send(tfull.at[c, y, h, l, :, :, :, cols], xin_t.at[k, :, :, :, cols], target))
        yield
        for copy in xs:
            copy.wait_recv()
        zs = []
        for k, (by, target) in enumerate(((2, zfar), (1, zup), (3, zdown), (0, None))):
            h, l = lax.div(turn(z, by), 2), lax.rem(turn(z, by), 2)
            mine = tfull.at[c, y, xh, xl, h, l, :, cols]
            terms = [xin_t.at[i, h, l, :, cols] for i in range(3)]
            if target is None:
                final = total([mine] + terms)
            else:
                add_to(mine, *terms)
                zs.append(send(mine, zin_t.at[k, :, cols], target))
        yield
        for copy in zs:
            copy.wait_recv()
        final = final + total([zin_t.at[i, :, cols] for i in range(3)])
        for b in range(PIECE // 128):
            block[col // 128 + b] = final[:, b * 128 : (b + 1) * 128]
        sent([s, r0, r1, y0, y1] + xs + zs)
        yield

    def hand_out():
        for r in range(2):
            for b in range(8):
                flat[pl.ds(r * 8 + b, 8, stride=16), :] = block[b, pl.ds(r, 8, stride=2), :]
        copies = []
        for step in range(1, 8):
            j = mate(step)
            copies.append(
                send(flat.at[pl.ds(pl.multiple_of(j * 16, 16), 16), :], gin.at[step], (sec, zh * 8 + j))
            )
        yield
        tgrad_ref[member] = flat[pl.ds(pl.multiple_of(member * 16, 16), 16), :]
        for step, copy in zip(range(1, 8), copies):
            copy.wait_recv()
            tgrad_ref[lax.rem(member + 8 - step, 8)] = gin[step]
        sent(copies)
        yield

    def go(*tasks):
        for task in tasks:
            next(task, None)

    queries[...] = jnp.zeros_like(queries)
    gradout[...] = jnp.zeros_like(gradout)

    tiles = gather_tiles()
    ha = [gather_xz(hfull, part, use_hidden) for part in XZ]
    hb = [gather_zx(hfull, part, use_hidden) for part in ZX]
    ca = [gather_xz(cfull, part, use_cot) for part in XZ]
    cb = [gather_zx(cfull, part, use_cot) for part in ZX]

    go(tiles)
    go(hb[0], ha[0], hb[1], ha[1])
    go(tiles)
    go(*ha)
    go(*hb)
    go(tiles)
    go(cb[0], ca[0], cb[1], ca[1])
    go(*ha)
    go(*hb)
    go(tiles)
    go(*ca)
    go(*hb)
    go(*ha)
    go(*cb)
    go(*ca)
    loads[0].wait()
    go(*hb)
    go(*ha)
    go(tiles)
    go(*cb)
    go(tiles)
    go(*cb)
    go(*ca)
    go(tiles)

    loads[1].wait()
    value = jnp.zeros((ROWS, HD), F32)
    for core in range(2):
        for h in range(2):
            for l in range(2):
                rows = tfull[core, :, h, :, :, l].reshape(ROWS, 1024)
                at = (l * 4 + h * 2 + core) * 1024
                value = value + jnp.dot(rows, wt[pl.ds(at, 1024), :], preferred_element_type=F32)
    proj[...] = value
    normed = value * norm_scale(value) * key_gain
    kv[c] = jnp.where(c == 0, normed, value).astype(BF)
    kv_copy = here(kv.at[c], sib)
    for h in range(HEADS):
        sl = pl.ds(h * HD, HD)
        q = queries[:, sl]
        normedq[:, sl] = (q * norm_scale(q) * query_gain).astype(BF)
    kv_copy.wait_recv()

    keys, values = kv[0], kv[1]
    for h in range(HEADS):
        sl = pl.ds(h * HD, HD)
        scores = contract_last(normedq[:, sl], keys)
        raised = jnp.where(mask[...] > 0.0, jnp.exp(scores), 0.0)
        w = (raised / jnp.sum(raised, axis=-1, keepdims=True)).astype(BF)
        weights[h] = w
        attended[:, sl] = jnp.dot(w, values, preferred_element_type=F32).astype(BF)

    loads[2].wait()
    oa = [scatter_xz(hfull, sib_o, rel_o, zin_o, xin_o, part, make_out, finish_out) for part in XZ]
    ob = [scatter_zx(hfull, sib_o, rel_o, zin_o, xin_o, part, make_out, finish_out) for part in ZX]
    go(ob[0], oa[0], ob[1], oa[1])
    go(*cb)
    go(*ca)
    go(ob[0], oa[0], ob[1], oa[1])

    grad_keys = jnp.zeros((ROWS, HD), F32)
    grad_values = jnp.zeros((ROWS, HD), F32)
    for h in range(HEADS):
        sl = pl.ds(h * HD, HD)
        g = (gate * gradout[:, sl]).astype(BF)
        w = weights[h]
        wide = w.astype(F32)
        prob = contract_last(g, values)
        score = (wide * (prob - jnp.sum(wide * prob, axis=-1, keepdims=True))).astype(BF)
        q = queries[:, sl]
        back = jnp.dot(score, keys, preferred_element_type=F32)
        gradq[:, sl] = head_norm_back(q, norm_scale(q), query_gain, back).astype(BF)
        grad_keys = grad_keys + contract_first(score, normedq[:, sl])
        grad_values = grad_values + contract_first(w, g)
    gxout[...] = jnp.where(c == 0, grad_values, grad_keys).astype(BF)
    gx_copy = send(gxout, gxin, sib)
    kept = jnp.where(c == 0, grad_keys, grad_values).astype(BF).astype(F32)
    go(oa[0], oa[1], ob[0], ob[1])
    gx_copy.wait()
    both = kept + gxin[...].astype(F32)
    raw = proj[...]
    gxout[...] = jnp.where(c == 0, head_norm_back(raw, norm_scale(raw), key_gain, both), both).astype(BF)

    ts = [scatter_tiles(col) for col in range(0, 1024, PIECE)]
    go(*ts)
    ga = [scatter_xz(cfull, sib_g, rel_g, zin_g, xin_g, part, make_grad, finish_grad) for part in XZ]
    gb = [scatter_zx(cfull, sib_g, rel_g, zin_g, xin_g, part, make_grad, finish_grad) for part in ZX]
    go(*ts)
    go(gb[0], ga[0], gb[1], ga[1])
    go(*ob)
    go(*oa)
    go(*ts)
    go(gb[0], ga[0], gb[1], ga[1])
    go(*ob)
    go(*oa)
    go(*ga)
    go(*gb)
    go(*ts)
    go(*ga)
    go(*gb)
    go(*ts)
    go(*ga)
    go(*gb)
    go(*ts)
    last = hand_out()
    go(last)
    go(last)
    kv_copy.wait_send()


def body(hidden, tiles, tile_counts, sample_order, query_weight, tile_weight, output_weight, head_gains, cross_gate, cotangent):
    til = tiles.reshape(2, 8, 8, 128).transpose(1, 0, 2, 3).reshape(8, 16, 128)
    smem = pl.BlockSpec(memory_space=pltpu.SMEM)
    vmem = pl.BlockSpec(memory_space=pltpu.VMEM)
    hbm = pl.BlockSpec(memory_space=pl.ANY)
    rows = (2, 4, 2, 16, D)

    def tp_buffers():
        return [
            pltpu.VMEM((4, 2, 16, D), BF),
            pltpu.VMEM((2, 2, 16, D), BF),
            pltpu.VMEM((2, 2, 16, D), BF),
            pltpu.VMEM((4, 16, D), BF),
        ]

    copies = 200
    out, grad, tgrad = pl.pallas_call(
        kernel,
        out_shape=(
            jax.ShapeDtypeStruct((16, D), BF),
            jax.ShapeDtypeStruct((16, D), BF),
            jax.ShapeDtypeStruct((8, 16, 128), F32),
        ),
        in_specs=[smem, smem, smem, vmem, vmem, vmem, vmem, hbm, hbm, hbm],
        out_specs=(vmem, vmem, vmem),
        scratch_shapes=[
            pltpu.VMEM((D, LOCAL), BF),
            pltpu.VMEM((D, HD), BF),
            pltpu.VMEM((LOCAL, D), BF),
            pltpu.VMEM(rows, BF),
            pltpu.VMEM(rows, BF),
            pltpu.VMEM((2, 4, 2, 2, 2, 2, 16, 1024), BF),
            *tp_buffers(),
            *tp_buffers(),
            pltpu.VMEM((4, 2, 2, 2, 2, 16, 1024), BF),
            pltpu.VMEM((2, 2, 2, 2, 16, 1024), BF),
            pltpu.VMEM((2, 2, 2, 2, 2, 16, 1024), BF),
            pltpu.VMEM((3, 2, 2, 16, 1024), BF),
            pltpu.VMEM((3, 16, 1024), BF),
            pltpu.VMEM((8, 16, 128), BF),
            pltpu.VMEM((128, 128), F32),
            pltpu.VMEM((8, 16, 128), F32),
            pltpu.VMEM((8, 16, 128), F32),
            pltpu.VMEM((ROWS, LOCAL), F32),
            pltpu.VMEM((ROWS, LOCAL), F32),
            pltpu.VMEM((ROWS, LOCAL), BF),
            pltpu.VMEM((HEADS, ROWS, ROWS), BF),
            pltpu.VMEM((ROWS, LOCAL), BF),
            pltpu.VMEM((ROWS, LOCAL), BF),
            pltpu.VMEM((ROWS, HD), F32),
            pltpu.VMEM((2, ROWS, HD), BF),
            pltpu.VMEM((ROWS, HD), BF),
            pltpu.VMEM((ROWS, HD), BF),
            pltpu.VMEM((ROWS, ROWS), F32),
            pltpu.SemaphoreType.DMA((3,)),
            pltpu.SemaphoreType.DMA((copies,)),
            pltpu.SemaphoreType.DMA((copies,)),
        ],
        compiler_params=pltpu.CompilerParams(
            collective_id=0, has_side_effects=True, vmem_limit_bytes=60 * 2**20
        ),
        name="cross_attention",
    )(
        tile_counts, sample_order, cross_gate, head_gains[0], hidden[0], cotangent[0], til,
        query_weight[0], tile_weight[0], output_weight[0],
    )
    tile_grad = tgrad.reshape(8, 2, 8, 128).transpose(1, 0, 2, 3).reshape(2, D)
    return (out[None], grad[None], tile_grad)


def solution(mesh):
    placed = (
        P("section", "tp", None),
        P(("section", "tp"), None),
        P(),
        P(),
        P("section", None, "tp"),
        P("section", None, "tp"),
        P("section", "tp", None),
        P("section", None, None),
        P("section"),
        P("section", "tp", None),
    )
    return jax.shard_map(
        body,
        mesh=mesh,
        in_specs=placed,
        out_specs=(P("section", "tp", None), P("section", "tp", None), P(("section", "tp"), None)),
        check_vma=False,
    )
```

time: 689 us -> 141 us (0.20)
  waiting for transfers between devices: 592 us -> 0 us
  Pallas kernels: 0 us -> 133 us
  matrix products: 50.5 us -> 0 us
  local copies, waits for them, and re-layouts: 22.1 us -> 6.24 us
  between operations: 15.1 us -> 1.29 us
    all_gather x3 -> x0, waiting for transfers between devices: 285 us -> none  [the longest x1 189 us: body(): lax.all_gather(tiles, ('section', 'tp'), axis=0, tiled=True)]
    reduce_scatter x2 -> x0, waiting for transfers between devices: 162 us -> none  [the longest x1 81.6 us: body(): lax.psum_scatter(contract_last(block, query_local).astype(jnp.bfloat16),...]
    unnamed x7 -> x0, waiting for transfers between devices: 143 us -> none
    pallas_call x0 -> x1, Pallas kernels: none -> 133 us  [body(): pl.pallas_call(kernel, out_shape=(jax.ShapeDtypeStruct((16, D), BF), jax....]
    dot_general x13 -> x0, matrix products: 49.2 us -> none  [the longest x4 22.7 us: contract_last(): lax.dot_general(left, right, (((1,), (1,)), ((), ())), preferred_element_...]
    dot_general x1 -> x0, local copies, waits for them, and re-layouts: 11.4 us -> none  [body(): jnp.dot(lax.all_gather(text_rows, 'tp', axis=0, tiled=True), query_local,...]
  transfers between devices with their start and end apart: 8 -> 0, of which waited for: 8 -> 0; matrix products, arithmetic and copies ran while one was open for 7% -> 0% of each run, Pallas kernels for 0% -> 0%
where the time goes in v1:
time: 141 us; the launch traced here: 140 us
  Pallas kernels  133 us (94%)
  local copies, waits for them, and re-layouts  6.24 us (4%)
    pallas_call x1, Pallas kernels, body(): pl.pallas_call(kernel, out_shape=(jax.ShapeDtypeStruct((16, D), BF), jax....  133 us
    unnamed x4, local copies, waits for them, and re-layouts  4.86 us

profile of v1, /device:TPU:1, one launch (start us, length us, event | category | flops | bytes accessed | tf_op | source)
XLA Modules:
  0.0 140.3 jit_solution(12682541137011927141)
XLA Ops:
  1.3 1.4 copy_bitcast_fusion.3.til
  2.7 132.7 %cross_attention.1 = (bf16[16,8192]{1,0:T(8,128)(2,1)}, bf16[16,8192]{1,0:T(8,128)(2,1)}, f32[8,16,128]{2,1,0:T(8,128)}) custom-call(s32[4]{0:T(128)} %counts.1, s32[4]{0:T(128)} %order.1, f32[1]{0:T(128)S(6)} %copy.25.gate_ref, f32[2,128]{1,0:T(2,128)} %bitcast.37, bf16[16,8192]{1,0:T(8,128)(2,1)} %bitcast.31, bf16[16,8192]{1,0:T(8,128)(2,1)} %bitcast.32, ...), custom_call_target="tpu_custom_call" | custom-call | tf_op jit(solution)/shard_map/cross_attention/pallas_call | solution.py:587
  135.4 0.8 copy_bitcast_fusion.1
  136.3 0.7 copy.22
  136.9 1.7 %copy.26 = bf16[1,16,8192]{2,1,0:T(8,128)(2,1)} copy(bf16[1,16,8192]{2,1,0:T(8,128)(2,1)} %bitcast.34) | data formatting | bytes 524288
  138.6 1.7 %copy.27 = bf16[1,16,8192]{2,1,0:T(8,128)(2,1)} copy(bf16[1,16,8192]{2,1,0:T(8,128)(2,1)} %bitcast.33) | data formatting | bytes 524288

commit v2 on v1

--- a/solution.py
+++ b/solution.py
@@ -16,9 +16,20 @@
 BF = jnp.bfloat16
 F32 = jnp.float32
 
-XZ = ((0, 2304, 768), (2304, 2304, 768))
-ZX = ((4608, 1792, 896), (6400, 1792, 896))
+XZ = ((0, 2560), (2560, 2560))
+ZX = ((5120, 1536), (6656, 1536))
 PIECE = 512
+
+ORDER = (
+    "ca0", "ha0", "ha1", "t", "hb0", "hb0", "ca1", "cb1", "cb1", "cb0", "hb1", "hb1", "cb0", "t",
+    "ca0", "hb0", "cb1", "ha0", "cb0", "hb1", "ha1", "t", "ca1", "ca0", "hb0", "cb1", "ha0", "cb0",
+    "hb1", "ha1", "t", "t", "ca1", "ca0", "t", "t", "ha0", "hb0", "ca0", "t", "cb1", "ha1", "cb0",
+    "ha0", "hb0", "ca1", "hb1", "t", "cb1", "ha1", "t", "cb0", "ca1", "hb1", "t", "t", "t", "bw",
+    "gb0", "oa1", "oa0", "gb0", "bw", "p1", "oa1", "ob1", "p0", "oa0", "ob0", "p1", "ob1", "oa1",
+    "ga1", "gb0", "p0", "oa0", "ob0", "ga0", "ga1", "p1", "gb1", "oa1", "gb0", "ob1", "ga0", "p0",
+    "gb1", "oa0", "ob0", "ga1", "oa1", "gb0", "p1", "ob1", "ga0", "ob0", "gb1", "p0", "ga1", "oa0",
+    "ob1", "p1", "ga0", "p0", "ob0", "gb1", "ga1", "p1", "p0", "l", "ga0", "gb1", "l",
+)
 
 
 def contract_last(left, right):
@@ -47,13 +58,13 @@
 
 
 def kernel(
-    counts, order, gate_ref, gains, hid, cot, til, wq_hbm, wt_hbm, wo_hbm,
+    counts, order, gate_ref, gains, hid, cot, tiles_ref, wq_hbm, wt_hbm, wo_hbm,
     out_ref, grad_ref, tgrad_ref,
     wq, wt, wo, hfull, cfull, tfull,
     sib_o, rel_o, zin_o, xin_o,
     sib_g, rel_g, zin_g, xin_g,
     sib_t, yrel, yin, xin_t, zin_t,
-    tin, flat, block, gin,
+    til, tin, flat, block, gin,
     queries, gradout, normedq, weights, attended, gradq, proj, kv, gxin, gxout, mask,
     load_sem, send_sem, recv_sem,
 ):
@@ -134,7 +145,7 @@
             copy.wait_send()
 
     def gather_xz(full, part, use):
-        col, width, _ = part
+        col, width = part
         cols = pl.ds(col, width)
         low, high = pl.ds(col, width // 2), pl.ds(col + width // 2, width // 2)
         a = here(full.at[c, z, xh, :, cols], xpair)
@@ -158,11 +169,13 @@
         yield
 
     def gather_zx(full, part, use):
-        col, width, _ = part
+        col, width = part
         cols = pl.ds(col, width)
         low, high = pl.ds(col, width // 2), pl.ds(col + width // 2, width // 2)
         mine = full.at[c, z, xh, :, cols]
-        up, down, a = here(mine, zup), here(mine, zdown), here(mine, xpair)
+        up, down = here(mine, zup), here(mine, zdown)
+        yield
+        a = here(mine, xpair)
         yield
         up.wait_recv()
         up2 = here(full.at[c, turn(z, 3), xh, :, low], zup)
@@ -184,32 +197,36 @@
         sent([up, down, a, up2, a1, down2, a2, a3, s])
         yield
 
+    loaded = set()
+
+    def need(i):
+        if i not in loaded:
+            loaded.add(i)
+            loads[i].wait()
+
     def use_hidden(part):
-        col, width, step = part
-
-        def one(i, carry):
-            at = pl.ds(pl.multiple_of(col + i * step, 128), step)
-            rows = hfull[:, :, :, :, at].reshape(ROWS, step)
-            queries[...] += jnp.dot(rows, wq[at, :], preferred_element_type=F32)
-            return carry
-
-        lax.fori_loop(0, width // step, one, 0)
+        need(0)
+        at = pl.ds(*part)
+        rows = hfull[:, :, :, :, at].reshape(ROWS, part[1])
+        queries[...] += jnp.dot(rows, wq[at, :], preferred_element_type=F32)
 
     def use_cot(part):
-        col, width, step = part
-
-        def one(i, carry):
-            at = pl.ds(pl.multiple_of(col + i * step, 128), step)
-            rows = cfull[:, :, :, :, at].reshape(ROWS, step)
-            gradout[...] += contract_last(rows, wo[:, at])
-            return carry
-
-        lax.fori_loop(0, width // step, one, 0)
+        need(2)
+        at = pl.ds(*part)
+        rows = cfull[:, :, :, :, at].reshape(ROWS, part[1])
+        gradout[...] += contract_last(rows, wo[:, at])
 
     def tblock(full, yy, xx):
         return full.at[c, yy, lax.div(xx, 2), lax.rem(xx, 2)]
 
     def gather_tiles():
+        wide = tiles_ref[...].astype(F32)
+        for j in range(8):
+            for b in range(8):
+                at = (j * 8 + b) * 128
+                flat[pl.ds(j * 16 + b, 2, stride=8), :] = wide[:, at : at + 128]
+        for j in range(8):
+            til[j] = flat[j * 16 : (j + 1) * 16, :].astype(BF)
         copies = []
         for step in range(1, 8):
             j = mate(step)
@@ -234,16 +251,16 @@
         mine = tblock(tfull, y, x)
         xs = [here(mine, xup), here(mine, xdown), here(mine, xpair)]
         ups, downs = [here(mine, yup)], [here(mine, ydown)]
-        yield
         for copy, by in zip(xs, (3, 1, 2)):
+            yield
             copy.wait_recv()
             got = tblock(tfull, y, turn(x, by))
             ups.append(here(got, yup))
             downs.append(here(got, ydown))
         sibs = [here(tfull.at[c, y], sib)]
-        yield
         far = []
         for k, by in enumerate((0, 3, 1, 2)):
+            yield
             ups[k].wait_recv()
             downs[k].wait_recv()
             if k % 2 == 0:
@@ -260,10 +277,11 @@
         for copy in sibs:
             copy.wait_recv()
         sent(copies + zs + xs + ups + downs + far + sibs)
+        yield from attend()
         yield
 
     def scatter_xz(full, sibin, rel, zin, xin, part, make, finish):
-        col, width, _ = part
+        col, width = part
         cols = pl.ds(col, width)
         low, high = pl.ds(col, width // 2), pl.ds(col + width // 2, width // 2)
         make(part)
@@ -294,7 +312,7 @@
         yield
 
     def scatter_zx(full, sibin, rel, zin, xin, part, make, finish):
-        col, width, _ = part
+        col, width = part
         cols = pl.ds(col, width)
         low, high = pl.ds(col, width // 2), pl.ds(col + width // 2, width // 2)
         make(part)
@@ -331,29 +349,17 @@
         return value
 
     def make_out(part):
-        col, width, _ = part
-
-        def one(i, carry):
-            at = pl.ds(pl.multiple_of(col + i * 256, 128), 256)
-            value = jnp.dot(attended[...], wo[:, at], preferred_element_type=F32)
-            hfull[:, :, :, :, at] = value.astype(BF).reshape(2, 4, 2, 16, 256)
-            return carry
-
-        lax.fori_loop(0, width // 256, one, 0)
+        at = pl.ds(*part)
+        value = jnp.dot(attended[...], wo[:, at], preferred_element_type=F32)
+        hfull[:, :, :, :, at] = value.astype(BF).reshape(2, 4, 2, 16, part[1])
 
     def finish_out(cols, terms):
         out_ref[:, cols] = (hid[:, cols].astype(F32) + gate[0:1, 0:1] * total(terms)).astype(BF)
 
     def make_grad(part):
-        col, width, _ = part
-
-        def one(i, carry):
-            at = pl.ds(pl.multiple_of(col + i * 256, 128), 256)
-            value = contract_last(gradq[...], wq[at, :])
-            cfull[:, :, :, :, at] = value.astype(BF).reshape(2, 4, 2, 16, 256)
-            return carry
-
-        lax.fori_loop(0, width // 256, one, 0)
+        at = pl.ds(*part)
+        value = contract_last(gradq[...], wq[at, :])
+        cfull[:, :, :, :, at] = value.astype(BF).reshape(2, 4, 2, 16, part[1])
 
     def finish_grad(cols, terms):
         grad_ref[:, cols] = (cot[:, cols].astype(F32) + total(terms)).astype(BF)
@@ -438,138 +444,94 @@
                 send(flat.at[pl.ds(pl.multiple_of(j * 16, 16), 16), :], gin.at[step], (sec, zh * 8 + j))
             )
         yield
-        tgrad_ref[member] = flat[pl.ds(pl.multiple_of(member * 16, 16), 16), :]
-        for step, copy in zip(range(1, 8), copies):
-            copy.wait_recv()
-            tgrad_ref[lax.rem(member + 8 - step, 8)] = gin[step]
+        gin[0] = flat[pl.ds(pl.multiple_of(member * 16, 16), 16), :]
+        for copy in copies:
+            copy.wait_recv()
         sent(copies)
-        yield
-
-    def go(*tasks):
-        for task in tasks:
-            next(task, None)
+        for s in range(8):
+            owner = lax.rem(member + 8 - s, 8)
+            flat[pl.ds(pl.multiple_of(owner * 16, 16), 16), :] = gin[s]
+        for j in range(8):
+            for b in range(8):
+                tgrad_ref[:, pl.ds((j * 8 + b) * 128, 128)] = flat[pl.ds(j * 16 + b, 2, stride=8), :]
+        yield
+
+    def attend():
+        need(1)
+        value = jnp.zeros((ROWS, HD), F32)
+        for core in range(2):
+            for h in range(2):
+                for l in range(2):
+                    rows = tfull[core, :, h, :, :, l].reshape(ROWS, 1024)
+                    at = (l * 4 + h * 2 + core) * 1024
+                    value = value + jnp.dot(rows, wt[pl.ds(at, 1024), :], preferred_element_type=F32)
+        proj[...] = value
+        normed = value * norm_scale(value) * key_gain
+        kv[c] = jnp.where(c == 0, normed, value).astype(BF)
+        kv_copy = here(kv.at[c], sib)
+        yield
+        for h in range(HEADS):
+            sl = pl.ds(h * HD, HD)
+            q = queries[:, sl]
+            normedq[:, sl] = (q * norm_scale(q) * query_gain).astype(BF)
+        kv_copy.wait_recv()
+
+        keys, values = kv[0], kv[1]
+        for h in range(HEADS):
+            sl = pl.ds(h * HD, HD)
+            scores = contract_last(normedq[:, sl], keys)
+            raised = jnp.where(mask[...] > 0.0, jnp.exp(scores), 0.0)
+            w = (raised / jnp.sum(raised, axis=-1, keepdims=True)).astype(BF)
+            weights[h] = w
+            attended[:, sl] = jnp.dot(w, values, preferred_element_type=F32).astype(BF)
+        kv_copy.wait_send()
+
+    def attend_back():
+        keys, values = kv[0], kv[1]
+        grad_keys = jnp.zeros((ROWS, HD), F32)
+        grad_values = jnp.zeros((ROWS, HD), F32)
+        for h in range(HEADS):
+            sl = pl.ds(h * HD, HD)
+            g = (gate * gradout[:, sl]).astype(BF)
+            w = weights[h]
+            wide = w.astype(F32)
+            prob = contract_last(g, values)
+            score = (wide * (prob - jnp.sum(wide * prob, axis=-1, keepdims=True))).astype(BF)
+            q = queries[:, sl]
+            back = jnp.dot(score, keys, preferred_element_type=F32)
+            gradq[:, sl] = head_norm_back(q, norm_scale(q), query_gain, back).astype(BF)
+            grad_keys = grad_keys + contract_first(score, normedq[:, sl])
+            grad_values = grad_values + contract_first(w, g)
+        gxout[...] = jnp.where(c == 0, grad_values, grad_keys).astype(BF)
+        gx_copy = send(gxout, gxin, sib)
+        kept = jnp.where(c == 0, grad_keys, grad_values).astype(BF).astype(F32)
+        yield
+        gx_copy.wait()
+        both = kept + gxin[...].astype(F32)
+        raw = proj[...]
+        gxout[...] = jnp.where(c == 0, head_norm_back(raw, norm_scale(raw), key_gain, both), both).astype(BF)
+        yield
 
     queries[...] = jnp.zeros_like(queries)
     gradout[...] = jnp.zeros_like(gradout)
 
-    tiles = gather_tiles()
-    ha = [gather_xz(hfull, part, use_hidden) for part in XZ]
-    hb = [gather_zx(hfull, part, use_hidden) for part in ZX]
-    ca = [gather_xz(cfull, part, use_cot) for part in XZ]
-    cb = [gather_zx(cfull, part, use_cot) for part in ZX]
-
-    go(tiles)
-    go(hb[0], ha[0], hb[1], ha[1])
-    go(tiles)
-    go(*ha)
-    go(*hb)
-    go(tiles)
-    go(cb[0], ca[0], cb[1], ca[1])
-    go(*ha)
-    go(*hb)
-    go(tiles)
-    go(*ca)
-    go(*hb)
-    go(*ha)
-    go(*cb)
-    go(*ca)
-    loads[0].wait()
-    go(*hb)
-    go(*ha)
-    go(tiles)
-    go(*cb)
-    go(tiles)
-    go(*cb)
-    go(*ca)
-    go(tiles)
-
-    loads[1].wait()
-    value = jnp.zeros((ROWS, HD), F32)
-    for core in range(2):
-        for h in range(2):
-            for l in range(2):
-                rows = tfull[core, :, h, :, :, l].reshape(ROWS, 1024)
-                at = (l * 4 + h * 2 + core) * 1024
-                value = value + jnp.dot(rows, wt[pl.ds(at, 1024), :], preferred_element_type=F32)
-    proj[...] = value
-    normed = value * norm_scale(value) * key_gain
-    kv[c] = jnp.where(c == 0, normed, value).astype(BF)
-    kv_copy = here(kv.at[c], sib)
-    for h in range(HEADS):
-        sl = pl.ds(h * HD, HD)
-        q = queries[:, sl]
-        normedq[:, sl] = (q * norm_scale(q) * query_gain).astype(BF)
-    kv_copy.wait_recv()
-
-    keys, values = kv[0], kv[1]
-    for h in range(HEADS):
-        sl = pl.ds(h * HD, HD)
-        scores = contract_last(normedq[:, sl], keys)
-        raised = jnp.where(mask[...] > 0.0, jnp.exp(scores), 0.0)
-        w = (raised / jnp.sum(raised, axis=-1, keepdims=True)).astype(BF)
-        weights[h] = w
-        attended[:, sl] = jnp.dot(w, values, preferred_element_type=F32).astype(BF)
-
-    loads[2].wait()
-    oa = [scatter_xz(hfull, sib_o, rel_o, zin_o, xin_o, part, make_out, finish_out) for part in XZ]
-    ob = [scatter_zx(hfull, sib_o, rel_o, zin_o, xin_o, part, make_out, finish_out) for part in ZX]
-    go(ob[0], oa[0], ob[1], oa[1])
-    go(*cb)
-    go(*ca)
-    go(ob[0], oa[0], ob[1], oa[1])
-
-    grad_keys = jnp.zeros((ROWS, HD), F32)
-    grad_values = jnp.zeros((ROWS, HD), F32)
-    for h in range(HEADS):
-        sl = pl.ds(h * HD, HD)
-        g = (gate * gradout[:, sl]).astype(BF)
-        w = weights[h]
-        wide = w.astype(F32)
-        prob = contract_last(g, values)
-        score = (wide * (prob - jnp.sum(wide * prob, axis=-1, keepdims=True))).astype(BF)
-        q = queries[:, sl]
-        back = jnp.dot(score, keys, preferred_element_type=F32)
-        gradq[:, sl] = head_norm_back(q, norm_scale(q), query_gain, back).astype(BF)
-        grad_keys = grad_keys + contract_first(score, normedq[:, sl])
-        grad_values = grad_values + contract_first(w, g)
-    gxout[...] = jnp.where(c == 0, grad_values, grad_keys).astype(BF)
-    gx_copy = send(gxout, gxin, sib)
-    kept = jnp.where(c == 0, grad_keys, grad_values).astype(BF).astype(F32)
-    go(oa[0], oa[1], ob[0], ob[1])
-    gx_copy.wait()
-    both = kept + gxin[...].astype(F32)
-    raw = proj[...]
-    gxout[...] = jnp.where(c == 0, head_norm_back(raw, norm_scale(raw), key_gain, both), both).astype(BF)
-
-    ts = [scatter_tiles(col) for col in range(0, 1024, PIECE)]
-    go(*ts)
-    ga = [scatter_xz(cfull, sib_g, rel_g, zin_g, xin_g, part, make_grad, finish_grad) for part in XZ]
-    gb = [scatter_zx(cfull, sib_g, rel_g, zin_g, xin_g, part, make_grad, finish_grad) for part in ZX]
-    go(*ts)
-    go(gb[0], ga[0], gb[1], ga[1])
-    go(*ob)
-    go(*oa)
-    go(*ts)
-    go(gb[0], ga[0], gb[1], ga[1])
-    go(*ob)
-    go(*oa)
-    go(*ga)
-    go(*gb)
-    go(*ts)
-    go(*ga)
-    go(*gb)
-    go(*ts)
-    go(*ga)
-    go(*gb)
-    go(*ts)
-    last = hand_out()
-    go(last)
-    go(last)
-    kv_copy.wait_send()
+    tasks = {"t": gather_tiles(), "bw": attend_back(), "l": hand_out()}
+    for i in range(2):
+        tasks["ha%d" % i] = gather_xz(hfull, XZ[i], use_hidden)
+        tasks["hb%d" % i] = gather_zx(hfull, ZX[i], use_hidden)
+        tasks["ca%d" % i] = gather_xz(cfull, XZ[i], use_cot)
+        tasks["cb%d" % i] = gather_zx(cfull, ZX[i], use_cot)
+        tasks["oa%d" % i] = scatter_xz(hfull, sib_o, rel_o, zin_o, xin_o, XZ[i], make_out, finish_out)
+        tasks["ob%d" % i] = scatter_zx(hfull, sib_o, rel_o, zin_o, xin_o, ZX[i], make_out, finish_out)
+        tasks["ga%d" % i] = scatter_xz(cfull, sib_g, rel_g, zin_g, xin_g, XZ[i], make_grad, finish_grad)
+        tasks["gb%d" % i] = scatter_zx(cfull, sib_g, rel_g, zin_g, xin_g, ZX[i], make_grad, finish_grad)
+    for i in range(1024 // PIECE):
+        tasks["p%d" % i] = scatter_tiles(i * PIECE)
+    for name in ORDER:
+        next(tasks[name])
 
 
 def body(hidden, tiles, tile_counts, sample_order, query_weight, tile_weight, output_weight, head_gains, cross_gate, cotangent):
-    til = tiles.reshape(2, 8, 8, 128).transpose(1, 0, 2, 3).reshape(8, 16, 128)
     smem = pl.BlockSpec(memory_space=pltpu.SMEM)
     vmem = pl.BlockSpec(memory_space=pltpu.VMEM)
     hbm = pl.BlockSpec(memory_space=pl.ANY)
@@ -589,7 +551,7 @@
         out_shape=(
             jax.ShapeDtypeStruct((16, D), BF),
             jax.ShapeDtypeStruct((16, D), BF),
-            jax.ShapeDtypeStruct((8, 16, 128), F32),
+            jax.ShapeDtypeStruct((2, D), F32),
         ),
         in_specs=[smem, smem, smem, vmem, vmem, vmem, vmem, hbm, hbm, hbm],
         out_specs=(vmem, vmem, vmem),
@@ -607,6 +569,7 @@
             pltpu.VMEM((2, 2, 2, 2, 2, 16, 1024), BF),
             pltpu.VMEM((3, 2, 2, 16, 1024), BF),
             pltpu.VMEM((3, 16, 1024), BF),
+            pltpu.VMEM((8, 16, 128), BF),
             pltpu.VMEM((8, 16, 128), BF),
             pltpu.VMEM((128, 128), F32),
             pltpu.VMEM((8, 16, 128), F32),
@@ -631,11 +594,10 @@
         ),
         name="cross_attention",
     )(
-        tile_counts, sample_order, cross_gate, head_gains[0], hidden[0], cotangent[0], til,
+        tile_counts, sample_order, cross_gate, head_gains[0], hidden[0], cotangent[0], tiles,
         query_weight[0], tile_weight[0], output_weight[0],
     )
-    tile_grad = tgrad.reshape(8, 2, 8, 128).transpose(1, 0, 2, 3).reshape(2, D)
-    return (out[None], grad[None], tile_grad)
+    return (out[None], grad[None], tgrad)
 
 
 def solution(mesh):

time: 141 us -> 108 us (0.77)
  Pallas kernels: 133 us -> 102 us
  local copies, waits for them, and re-layouts: 6.24 us -> 4.81 us
    pallas_call x1, Pallas kernels: 133 us -> 102 us  [body(): pl.pallas_call(kernel, out_shape=(jax.ShapeDtypeStruct((16, D), BF), jax....]
    unnamed x4 -> x3, local copies, waits for them, and re-layouts: 4.86 us -> 4.81 us
where the time goes in v2:
time: 108 us
  Pallas kernels  102 us (94%)
  local copies, waits for them, and re-layouts  4.81 us (4%)
  between operations  1.29 us (1%)
    pallas_call x1, Pallas kernels, body(): pl.pallas_call(kernel, out_shape=(jax.ShapeDtypeStruct((16, D), BF), jax....  102 us
    unnamed x3, local copies, waits for them, and re-layouts  4.81 us

profile of v2, /device:TPU:1, one launch (start us, length us, event | category | flops | bytes accessed | tf_op | source)
XLA Modules:
  0.0 107.9 jit_solution(12804355751871012468)
XLA Ops:
  1.3 101.8 %cross_attention.1 = (bf16[16,8192]{1,0:T(8,128)(2,1)}, bf16[16,8192]{1,0:T(8,128)(2,1)}, f32[2,8192]{1,0:T(2,128)}) custom-call(s32[4]{0:T(128)} %counts.1, s32[4]{0:T(128)} %order.1, f32[1]{0:T(128)S(6)} %copy.16.gate_ref, f32[2,128]{1,0:T(2,128)} %bitcast.15, bf16[16,8192]{1,0:T(8,128)(2,1)} %bitcast.11, bf16[16,8192]{1,0:T(8,128)(2,1)} %bitcast.12, ...), custom_call_target="tpu_custom_call" | custom-call | tf_op jit(solution)/shard_map/cross_attention/pallas_call | solution.py:549
  103.1 1.7 %copy.17 = bf16[1,16,8192]{2,1,0:T(8,128)(2,1)} copy(bf16[1,16,8192]{2,1,0:T(8,128)(2,1)} %bitcast.14) | data formatting | bytes 524288
  104.8 1.7 %copy.18 = bf16[1,16,8192]{2,1,0:T(8,128)(2,1)} copy(bf16[1,16,8192]{2,1,0:T(8,128)(2,1)} %bitcast.13) | data formatting | bytes 524288
  106.5 1.5 %copy.19 = f32[2,8192]{1,0:T(2,128)} copy(f32[2,8192]{1,0:T(2,128)} %get-tuple-element.14) | data formatting | bytes 131072

commit v3 on v2

--- a/solution.py
+++ b/solution.py
@@ -18,17 +18,18 @@
 
 XZ = ((0, 2560), (2560, 2560))
 ZX = ((5120, 1536), (6656, 1536))
-PIECE = 512
+PIECE = 256
 
 ORDER = (
-    "ca0", "ha0", "ha1", "t", "hb0", "hb0", "ca1", "cb1", "cb1", "cb0", "hb1", "hb1", "cb0", "t",
-    "ca0", "hb0", "cb1", "ha0", "cb0", "hb1", "ha1", "t", "ca1", "ca0", "hb0", "cb1", "ha0", "cb0",
-    "hb1", "ha1", "t", "t", "ca1", "ca0", "t", "t", "ha0", "hb0", "ca0", "t", "cb1", "ha1", "cb0",
-    "ha0", "hb0", "ca1", "hb1", "t", "cb1", "ha1", "t", "cb0", "ca1", "hb1", "t", "t", "t", "bw",
-    "gb0", "oa1", "oa0", "gb0", "bw", "p1", "oa1", "ob1", "p0", "oa0", "ob0", "p1", "ob1", "oa1",
-    "ga1", "gb0", "p0", "oa0", "ob0", "ga0", "ga1", "p1", "gb1", "oa1", "gb0", "ob1", "ga0", "p0",
-    "gb1", "oa0", "ob0", "ga1", "oa1", "gb0", "p1", "ob1", "ga0", "ob0", "gb1", "p0", "ga1", "oa0",
-    "ob1", "p1", "ga0", "p0", "ob0", "gb1", "ga1", "p1", "p0", "l", "ga0", "gb1", "l",
+    "t", "ca1", "ca0", "cb0", "hb0", "t", "ha1", "cb0", "cb1", "ca1", "hb0", "t", "hb0", "ca0",
+    "ha1", "hb0", "t", "ca1", "ha0", "t", "cb0", "ca0", "t", "cb1", "hb1", "t", "hb0", "cb1", "t",
+    "ca1", "ha0", "ca0", "hb0", "t", "hb1", "cb0", "t", "cb1", "hb1", "ha1", "ca0", "ha0", "hb1",
+    "ca1", "cb0", "cb1", "ha1", "t", "ha0", "cb0", "cb1", "hb1", "ha1", "t", "ha0", "hb1", "t",
+    "ob1", "bw", "oa0", "ga0", "gb0", "ob1", "bw", "d", "oa0", "ga1", "ga0", "d", "p0", "gb1", "p1",
+    "gb0", "oa0", "ob0", "p3", "ob1", "oa1", "p2", "ob0", "ga1", "gb1", "p0", "oa1", "p3", "p1",
+    "gb0", "ob1", "ga1", "p0", "p2", "oa1", "oa0", "ob0", "p3", "p0", "gb1", "ga0", "p1", "p2",
+    "ob1", "ob0", "ga1", "oa1", "p3", "p1", "oa0", "p2", "gb1", "gb0", "ga0", "ga1", "p0", "p3",
+    "p1", "p2", "l", "ob0", "oa1", "gb0", "gb1", "ga0", "l",
 )
 
 
@@ -273,6 +274,8 @@
         for copy in far:
             copy.wait_recv()
         sibs.append(here(tfull.at[c, turn(y, 2)], sib))
+        need(1)
+        proj[...] = project(c)
         yield
         for copy in sibs:
             copy.wait_recv()
@@ -364,21 +367,30 @@
     def finish_grad(cols, terms):
         grad_ref[:, cols] = (cot[:, cols].astype(F32) + total(terms)).astype(BF)
 
-    def scatter_tiles(col):
-        cols = pl.ds(col, PIECE)
-
-        def unit(ref, *index):
-            return ref.at[(*index, Ellipsis, cols)]
-
+    tile_sibs = []
+
+    def make_tiles():
         for core in (oc, c):
             for h in range(2):
                 for l in range(2):
-                    at = (l * 4 + h * 2 + core) * 1024 + col
-                    value = contract_last(gxout[...], wt[pl.ds(pl.multiple_of(at, 128), PIECE), :])
-                    tfull[core, :, h, :, :, l, :, cols] = value.astype(BF).reshape(4, 2, 2, 16, PIECE)
+                    at = pl.multiple_of((l * 4 + h * 2 + core) * 1024, 1024)
+                    value = contract_last(gxout[...], wt[pl.ds(at, 1024), :])
+                    tfull[core, :, h, :, :, l] = value.astype(BF).reshape(4, 2, 2, 16, 1024)
             if core is oc:
-                s = send(tfull.at[oc, :, :, :, :, :, :, cols], sib_t.at[:, :, :, :, :, :, cols], sib)
-        yield
+                for col in range(0, 1024, PIECE):
+                    cols = pl.ds(col, PIECE)
+                    tile_sibs.append(
+                        send(tfull.at[oc, :, :, :, :, :, :, cols], sib_t.at[:, :, :, :, :, :, cols], sib)
+                    )
+            yield
+
+    def scatter_tiles(col):
+        cols = pl.ds(col, PIECE)
+
+        def unit(ref, *index):
+            return ref.at[(*index, Ellipsis, cols)]
+
+        s = tile_sibs[col // PIECE]
         s.wait_recv()
 
         def merge(by):
@@ -456,15 +468,17 @@
                 tgrad_ref[:, pl.ds((j * 8 + b) * 128, 128)] = flat[pl.ds(j * 16 + b, 2, stride=8), :]
         yield
 
+    def project(core):
+        value = jnp.zeros((ROWS, HD), F32)
+        for h in range(2):
+            for l in range(2):
+                rows = tfull[core, :, h, :, :, l].reshape(ROWS, 1024)
+                at = pl.multiple_of((l * 4 + h * 2 + core) * 1024, 1024)
+                value = value + jnp.dot(rows, wt[pl.ds(at, 1024), :], preferred_element_type=F32)
+        return value
+
     def attend():
-        need(1)
-        value = jnp.zeros((ROWS, HD), F32)
-        for core in range(2):
-            for h in range(2):
-                for l in range(2):
-                    rows = tfull[core, :, h, :, :, l].reshape(ROWS, 1024)
-                    at = (l * 4 + h * 2 + core) * 1024
-                    value = value + jnp.dot(rows, wt[pl.ds(at, 1024), :], preferred_element_type=F32)
+        value = proj[...] + project(oc)
         proj[...] = value
         normed = value * norm_scale(value) * key_gain
         kv[c] = jnp.where(c == 0, normed, value).astype(BF)
@@ -515,7 +529,7 @@
     queries[...] = jnp.zeros_like(queries)
     gradout[...] = jnp.zeros_like(gradout)
 
-    tasks = {"t": gather_tiles(), "bw": attend_back(), "l": hand_out()}
+    tasks = {"t": gather_tiles(), "bw": attend_back(), "d": make_tiles(), "l": hand_out()}
     for i in range(2):
         tasks["ha%d" % i] = gather_xz(hfull, XZ[i], use_hidden)
         tasks["hb%d" % i] = gather_zx(hfull, ZX[i], use_hidden)
@@ -545,7 +559,7 @@
             pltpu.VMEM((4, 16, D), BF),
         ]
 
-    copies = 200
+    copies = 224
     out, grad, tgrad = pl.pallas_call(
         kernel,
         out_shape=(

time: 108 us -> 106 us (0.981); the launches traced: 108 us -> 104 us
  Pallas kernels: 102 us -> 98 us
    pallas_call x1, Pallas kernels: 102 us -> 98 us  [body(): pl.pallas_call(kernel, out_shape=(jax.ShapeDtypeStruct((16, D), BF), jax....]
where the time goes in v3:
time: 106 us; the launch traced here: 104 us
  Pallas kernels  98 us (92%)
  local copies, waits for them, and re-layouts  4.81 us (5%)
  between operations  1.29 us (1%)
    pallas_call x1, Pallas kernels, body(): pl.pallas_call(kernel, out_shape=(jax.ShapeDtypeStruct((16, D), BF), jax....  98 us
    unnamed x3, local copies, waits for them, and re-layouts  4.81 us

profile of v3, /device:TPU:1, one launch (start us, length us, event | category | flops | bytes accessed | tf_op | source)
XLA Modules:
  0.0 104.1 jit_solution(3516493165408342772)
XLA Ops:
  1.3 98.0 %cross_attention.1 = (bf16[16,8192]{1,0:T(8,128)(2,1)}, bf16[16,8192]{1,0:T(8,128)(2,1)}, f32[2,8192]{1,0:T(2,128)}) custom-call(s32[4]{0:T(128)} %counts.1, s32[4]{0:T(128)} %order.1, f32[1]{0:T(128)S(6)} %copy.16.gate_ref, f32[2,128]{1,0:T(2,128)} %bitcast.15, bf16[16,8192]{1,0:T(8,128)(2,1)} %bitcast.11, bf16[16,8192]{1,0:T(8,128)(2,1)} %bitcast.12, ...), custom_call_target="tpu_custom_call" | custom-call | tf_op jit(solution)/shard_map/cross_attention/pallas_call | solution.py:563
  99.3 1.7 %copy.17 = bf16[1,16,8192]{2,1,0:T(8,128)(2,1)} copy(bf16[1,16,8192]{2,1,0:T(8,128)(2,1)} %bitcast.14) | data formatting | bytes 524288
  101.0 1.7 %copy.18 = bf16[1,16,8192]{2,1,0:T(8,128)(2,1)} copy(bf16[1,16,8192]{2,1,0:T(8,128)(2,1)} %bitcast.13) | data formatting | bytes 524288
  102.7 1.5 %copy.19 = f32[2,8192]{1,0:T(2,128)} copy(f32[2,8192]{1,0:T(2,128)} %get-tuple-element.14) | data formatting | bytes 131072

commit v4 on v3

--- a/solution.py
+++ b/solution.py
@@ -124,6 +124,16 @@
     query_gain = gains[0:1, :] * HD ** (-0.5)
     key_gain = gains[1:2, :]
 
+    queries[...] = jnp.zeros_like(queries)
+    gradout[...] = jnp.zeros_like(gradout)
+    wide = tiles_ref[...].astype(F32)
+    for j in range(8):
+        for b in range(8):
+            at = (j * 8 + b) * 128
+            flat[pl.ds(j * 16 + b, 2, stride=8), :] = wide[:, at : at + 128]
+    for j in range(8):
+        til[j] = flat[j * 16 : (j + 1) * 16, :].astype(BF)
+
     pl.semaphore_wait(barrier, len(greeted))
 
     used = [0]
@@ -221,13 +231,6 @@
         return full.at[c, yy, lax.div(xx, 2), lax.rem(xx, 2)]
 
     def gather_tiles():
-        wide = tiles_ref[...].astype(F32)
-        for j in range(8):
-            for b in range(8):
-                at = (j * 8 + b) * 128
-                flat[pl.ds(j * 16 + b, 2, stride=8), :] = wide[:, at : at + 128]
-        for j in range(8):
-            til[j] = flat[j * 16 : (j + 1) * 16, :].astype(BF)
         copies = []
         for step in range(1, 8):
             j = mate(step)
@@ -271,9 +274,9 @@
         sibs.append(here(tfull.at[c, turn(y, 3)], sib))
         sibs.append(here(tfull.at[c, turn(y, 1)], sib))
         yield
-        for copy in far:
-            copy.wait_recv()
-        sibs.append(here(tfull.at[c, turn(y, 2)], sib))
+        for copy, by in zip(far, (0, 3, 1, 2)):
+            copy.wait_recv()
+            sibs.append(here(tblock(tfull, turn(y, 2), turn(x, by)), sib))
         need(1)
         proj[...] = project(c)
         yield
@@ -525,9 +528,6 @@
         raw = proj[...]
         gxout[...] = jnp.where(c == 0, head_norm_back(raw, norm_scale(raw), key_gain, both), both).astype(BF)
         yield
-
-    queries[...] = jnp.zeros_like(queries)
-    gradout[...] = jnp.zeros_like(gradout)
 
     tasks = {"t": gather_tiles(), "bw": attend_back(), "d": make_tiles(), "l": hand_out()}
     for i in range(2):

time: 106 us -> 105 us (level)
  no operation moved by 1% of the time
where the time goes in v4:
time: 105 us; the launch traced here: 104 us
  Pallas kernels  98 us (93%)
  local copies, waits for them, and re-layouts  4.81 us (5%)
  between operations  1.29 us (1%)
    pallas_call x1, Pallas kernels, body(): pl.pallas_call(kernel, out_shape=(jax.ShapeDtypeStruct((16, D), BF), jax....  98 us
    unnamed x3, local copies, waits for them, and re-layouts  4.81 us

profile of v4, /device:TPU:1, one launch (start us, length us, event | category | flops | bytes accessed | tf_op | source)
XLA Modules:
  0.0 104.1 jit_solution(8906263435224531807)
XLA Ops:
  1.3 98.0 %cross_attention.1 = (bf16[16,8192]{1,0:T(8,128)(2,1)}, bf16[16,8192]{1,0:T(8,128)(2,1)}, f32[2,8192]{1,0:T(2,128)}) custom-call(s32[4]{0:T(128)} %counts.1, s32[4]{0:T(128)} %order.1, f32[1]{0:T(128)S(6)} %copy.16.gate_ref, f32[2,128]{1,0:T(2,128)} %bitcast.15, bf16[16,8192]{1,0:T(8,128)(2,1)} %bitcast.11, bf16[16,8192]{1,0:T(8,128)(2,1)} %bitcast.12, ...), custom_call_target="tpu_custom_call" | custom-call | tf_op jit(solution)/shard_map/cross_attention/pallas_call | solution.py:563
  99.3 1.7 %copy.17 = bf16[1,16,8192]{2,1,0:T(8,128)(2,1)} copy(bf16[1,16,8192]{2,1,0:T(8,128)(2,1)} %bitcast.14) | data formatting | bytes 524288
  101.0 1.7 %copy.18 = bf16[1,16,8192]{2,1,0:T(8,128)(2,1)} copy(bf16[1,16,8192]{2,1,0:T(8,128)(2,1)} %bitcast.13) | data formatting | bytes 524288
  102.6 1.5 %copy.19 = f32[2,8192]{1,0:T(2,128)} copy(f32[2,8192]{1,0:T(2,128)} %get-tuple-element.14) | data formatting | bytes 131072
